TPU v7x, 128 devices: a whole 4x4x4 slice. The times are simulated.
128 devices in a mesh: gx: 16 (over z, y), gy: 8 (over x, core).
Axes of the slice: x: 4, y: 4, z: 4, core: 2. Of those that a mesh axis runs over, the one named last changes fastest.
Arguments:
- nest_field: float32 [96, 256, 1024], P(None, 'gx', 'gy'), may hold values from -6 to 6
- courant_x: float32 [96, 256, 1024], P(None, 'gx', 'gy'), may hold values from -0.35 to 0.35
- courant_y: float32 [96, 256, 1024], P(None, 'gx', 'gy'), may hold values from -0.35 to 0.35
- courant_z: float32 [96, 256, 1024], P(None, 'gx', 'gy'), may hold values from -0.25 to 0.25
- terrain: int32 [256, 1024], P('gx', 'gy'), may hold values from 0 to 31
- relax: float32 [256, 1024], P('gx', 'gy'), may hold values from 0.1 to 0.6
- interp_index: int32 [4, 256, 1024], P(None, 'gx', 'gy'), may hold values from 0 to 32767, as said below
- interp_weight: float32 [4, 256, 1024], P(None, 'gx', 'gy'), may hold values from 0.05 to 0.5
- send_slots: int32 [128, 256], P(('gx', 'gy')), may hold values from 0 to 32, as said below
- parent_field: float32 [96, 512, 1024], P(None, 'gx', 'gy'), may hold values from -6 to 6
- parent_cx: float32 [96, 512, 1024], P(None, 'gx', 'gy'), may hold values from -0.45 to 0.45
- parent_cy: float32 [96, 512, 1024], P(None, 'gx', 'gy'), may hold values from -0.45 to 0.45
- fb_index: int32 [128, 256, 81], P(('gx', 'gy')), may hold values from 0 to 2047
- fb_slot: int32 [128, 512], P(('gx', 'gy')), may hold values from 0 to 256, as said below
- fb_target: int32 [128, 512], P(('gx', 'gy')), may hold values from 0 to 4096, as said below
Outputs:
- nest_out: float32 [96, 256, 1024], P(None, 'gx', 'gy')
- parent_out: float32 [96, 512, 1024], P(None, 'gx', 'gy')
Inputs may be any that keep to these rules, and one draw needn't show every extreme that they name: `send_slots`: index 32 marks an empty slot; the rest name slabs of the sender. Slots to one owner are filled from the first. One busy nest owner gets all 2 slots full from every device; each device sends at least one slab to itself. `interp_index`: every index points at a column of a filled slot received by the column's own device; the four indices of a column lie in one slot, at consecutive columns of the slab (cyclically). `fb_slot`: index 256 marks an empty slot; each of a device's rows stands in at most one slot. One busy parent owner receives all 4 slots full from every device. `fb_target`: A slot's target is 4096 exactly where the sender left that slot empty; targets may repeat.
All inputs are finite; a program needn't handle non-finite values.
Results may differ from a plain program's by a relative error of at most 0.0003.
Values sent between devices are 32-bit elements; how exact they have to be, the bound alone decides.
A program may use at most 128 MiB of HBM per device.

v0:
```python
import functools

import jax
import jax.numpy as jnp
from jax import lax
from jax.experimental import pallas as pl
from jax.experimental.pallas import tpu as pltpu
from jax.sharding import PartitionSpec as P

TILE = 128
CAP = 2
FCAP = 4
SUBSTEPS = 3


blend_rate = 0.5


def extended(block, sides, width):
    for axis, dim in sides:
        count = lax.axis_size(axis)
        forward = [(i, i + 1) for i in range(count - 1)]
        backward = [(target, source) for source, target in forward]
        low = lax.ppermute(
            lax.slice_in_dim(block, block.shape[dim] - width, None, axis=dim), axis, forward
        )
        high = lax.ppermute(lax.slice_in_dim(block, 0, width, axis=dim), axis, backward)
        block = jnp.concatenate([low, block, high], axis=dim)
    return block


def upwind(padded, field, cx, cy):
    west = padded[:, :-2, 1:-1]
    east = padded[:, 2:, 1:-1]
    south = padded[:, 1:-1, :-2]
    north = padded[:, 1:-1, 2:]
    return cx * jnp.where(cx > 0, field - west, east - field) + cy * jnp.where(
        cy > 0, field - south, north - field
    )


def vertical(field, cz, mask):
    below = jnp.concatenate([field[:1], field[:-1]], axis=0)
    mask_below = jnp.concatenate([jnp.zeros_like(mask[:1]), mask[:-1]], axis=0)
    below = jnp.where(mask_below, below, field)
    above = jnp.concatenate([field[1:], field[-1:]], axis=0)
    return cz * jnp.where(cz > 0, field - below, above - field)


def dense_step(
    nest_field,
    courant_x,
    courant_y,
    courant_z,
    terrain,
    relax,
    interp_index,
    interp_weight,
    send_slots,
    parent_field,
    parent_cx,
    parent_cy,
    fb_index,
    fb_slot,
    fb_target,
):
    n_east = lax.axis_size("gx")
    n_north = lax.axis_size("gy")
    devices = n_east * n_north
    levels, nest_x, nest_y = nest_field.shape
    parent_x, parent_y = (parent_field.shape[1], parent_field.shape[2])
    parent_cols = parent_x * parent_y
    nest_cols = nest_x * nest_y
    slabs = parent_field
    slabs = jnp.concatenate([slabs, jnp.zeros((levels, 1, TILE), jnp.float32)], axis=1)
    picked = jnp.take(slabs, send_slots[0], axis=1)
    outgoing = picked.reshape(levels, devices, CAP, TILE)
    incoming = lax.all_to_all(outgoing, ("gx", "gy"), split_axis=1, concat_axis=1, tiled=True)
    received_cols = incoming.reshape(levels, -1).T
    padded_parent = extended(parent_field, (("gx", 1), ("gy", 2)), 1)
    advected = parent_field - upwind(padded_parent, parent_field, parent_cx, parent_cy)
    index_flat = interp_index.reshape(4, -1)
    weight_flat = interp_weight.reshape(4, -1)
    boundary_cols = weight_flat[0][:, None] * jnp.take(received_cols, index_flat[0], axis=0)
    for j in range(1, 4):
        boundary_cols = boundary_cols + weight_flat[j][:, None] * jnp.take(
            received_cols, index_flat[j], axis=0
        )
    boundary = boundary_cols.T.reshape(levels, nest_x, nest_y)
    level_ids = lax.broadcasted_iota(jnp.int32, (levels, 1, 1), 0)
    mask = level_ids >= terrain[None]
    field = jnp.where(mask, nest_field, 0.0)
    for step in range(SUBSTEPS):
        padded = extended(field, (("gx", 1), ("gy", 2)), 1)
        adv = field - upwind(padded, field, courant_x, courant_y) - vertical(field, courant_z, mask)
        field = jnp.where(mask, adv + relax[None] * (boundary - adv), 0.0)
    flat_nest = field.reshape(levels, nest_cols)
    row_count = fb_index.shape[1]
    averaged = fb_index.shape[2]
    row_ids = lax.broadcasted_iota(jnp.int32, (row_count, averaged), 0)
    averaging = jnp.zeros((row_count + 1, nest_cols), jnp.float32)
    averaging = averaging.at[row_ids, fb_index[0]].add(1.0 / averaged)
    slot_weights = jnp.take(averaging, fb_slot[0], axis=0)
    chosen_rows = lax.dot_general(
        slot_weights,
        flat_nest,
        (((1,), (1,)), ((), ())),
        precision=lax.Precision.HIGHEST,
        preferred_element_type=jnp.float32,
    )
    sending = chosen_rows.reshape(devices, FCAP * levels)
    arrived = lax.all_to_all(sending, ("gx", "gy"), split_axis=0, concat_axis=0, tiled=True)
    values = arrived.reshape(-1, levels)
    flat_parent = advected.reshape(levels, parent_cols)
    target = fb_target[0]
    current = jnp.take(flat_parent, jnp.minimum(target, parent_cols - 1), axis=1)
    delta = blend_rate * (values.T - current)
    updated = flat_parent.at[:, target].add(delta, mode="drop")
    return (field, updated.reshape(levels, parent_x, parent_y))


MESH = pl.DeviceIdType.MESH
LEV = 96
NX = 16
PXN = 32
KREQ = 64
GROUPS = 8
F32 = jnp.float32
BF16 = jnp.bfloat16
NT = (((1,), (1,)), ((), ()))


def halves(value):
    high = value.astype(BF16)
    return high, (value - high.astype(F32)).astype(BF16)


def step_kernel(
    slots_ref,
    nest_ref,
    cx_ref,
    cy_ref,
    cz_ref,
    terrain_ref,
    relax_ref,
    index_ref,
    weight_ref,
    parent_ref,
    pcx_ref,
    pcy_ref,
    fbi_ref,
    fbs_ref,
    fbt_ref,
    nest_out,
    parent_out,
    flag_out,
    q0,
    q1,
    q2,
    ybuf,
    ypack,
    adv1,
    bound,
    pq,
    pys,
    pyk,
    keep,
    shi,
    slo,
    req,
    reqin,
    ans,
    ansin,
    xmat,
    counts,
    cmat,
    qmat,
    tmat,
    fbsend,
    fbin,
    hotm,
    tabm,
    rankm,
    relm,
    nraw,
    cxs,
    cys,
    czs,
    pcxs,
    pcys,
    nres,
    fbt,
    fbn,
    sem_in,
    sem_out,
    sem_req_s,
    sem_req_r,
    sem_ans_s,
    sem_ans_r,
    sem_fb_s,
    sem_fb_r,
    hs,
    hr,
):
    gx = lax.axis_index("gx")
    gy = lax.axis_index("gy")
    mz, my, mx, mc = lax.div(gx, 4), lax.rem(gx, 4), lax.div(gy, 2), lax.rem(gy, 2)
    me = gx * 8 + gy

    def chip(n, sign):
        dx = lax.rem(n, 4)
        dy = lax.rem(lax.div(n, 4) + dx, 4)
        dz = lax.rem(lax.div(n, 16) + dy, 4)
        if sign < 0:
            dz, dy, dx = 4 - dz, 4 - dy, 4 - dx
        z, y, x = lax.rem(mz + dz, 4), lax.rem(my + dy, 4), lax.rem(mx + dx, 4)
        return z * 4 + y, x * 2

    barrier = pltpu.get_barrier_semaphore()

    def greet(n, carry):
        tx, ty = chip(n, 1)
        for core in range(2):
            pl.semaphore_signal(barrier, inc=1, device_id=(tx, ty + core), device_id_type=MESH)
        return carry

    lax.fori_loop(1, 64, greet, 0)
    pl.semaphore_signal(barrier, inc=1, device_id=(gx, mx * 2 + 1 - mc), device_id_type=MESH)

    def load(source, count, target, first, k):
        def one(x, carry):
            pltpu.make_async_copy(source.at[:, x], target.at[x + first], sem_in.at[k]).start()
            return carry

        lax.fori_loop(0, count, one, 0)

    def loaded(target, first, count, k):
        part = target.at[pl.ds(first, count)]
        pltpu.make_async_copy(part, part, sem_in.at[k]).wait()

    sub128 = lax.broadcasted_iota(jnp.int32, (128, 128), 0)
    lane128 = lax.broadcasted_iota(jnp.int32, (128, 128), 1)
    sub64 = lax.broadcasted_iota(jnp.int32, (KREQ, 128), 0)

    before = jnp.concatenate(
        [jnp.where(sub128 < lane128, 1.0, 0.0), jnp.ones((128, 128), F32)], axis=1
    ).astype(BF16)
    run = jnp.zeros((128, 128), F32)
    top = jnp.zeros((1, 128), F32)
    for x in range(NX):
        idx = [index_ref[j, x : x + 1, :] for j in range(4)]
        src = idx[0] >> 8
        dz, dy, dx = (src >> 5) - mz, ((src >> 3) & 3) - my, ((src >> 1) & 3) - mx
        rel = (((dz - dy) & 3) << 5) | (((dy - dx) & 3) << 3) | ((dx & 3) << 1) | (src & 1)
        relm[x : x + 1, :] = rel
        hot = jnp.where(sub128 == rel, 1.0, 0.0)
        hotb = hot.astype(BF16)
        both = jnp.dot(hotb, before, preferred_element_type=F32)
        rank = jnp.sum(hot * (both[:, :128] + run), axis=0, keepdims=True)
        run = run + both[:, 128:]
        top = jnp.maximum(top, rank)
        here = sub64 == rank.astype(jnp.int32)
        rankm[x] = jnp.where(here, 1.0, 0.0).astype(BF16)
        at = slice(128 * x, 128 * x + 128)
        hotm[:, at] = hotb
        for j in range(4):
            low = (idx[j] & 255).astype(F32)
            w = weight_ref[j, x : x + 1, :]
            whi = w.astype(BF16).astype(F32)
            tabm[128 * j : 128 * j + 64, at] = jnp.where(here, low, 0.0).astype(BF16)
            tabm[128 * j + 64 : 128 * j + 128, at] = jnp.where(here, whi, 0.0).astype(BF16)
            tabm[512 + 128 * j : 576 + 128 * j, at] = jnp.zeros((KREQ, 128), BF16)
            tabm[576 + 128 * j : 640 + 128 * j, at] = jnp.where(here, w - whi, 0.0).astype(BF16)
    flag = jnp.max(jnp.where(top >= KREQ, 1.0, 0.0), axis=1, keepdims=True)
    racc = lax.dot_general(hotm[...], tabm[...], NT, preferred_element_type=F32)
    for j in range(4):
        req[:, j, :] = (
            racc[:, 128 * j : 128 * j + 128] + racc[:, 512 + 128 * j : 640 + 128 * j]
        )

    load(parent_ref, PXN, pq, 1, 0)
    load(nest_ref, NX, nraw, 0, 1)
    pl.semaphore_wait(barrier, 127)

    def ask(n, carry):
        tx, ty = chip(n, 1)
        for core in range(2):
            pltpu.make_async_remote_copy(
                src_ref=req.at[2 * n + core],
                dst_ref=reqin.at[2 * n + mc],
                send_sem=sem_req_s,
                recv_sem=sem_req_r.at[lax.div(n, 64 // GROUPS)],
                device_id=(tx, ty + core),
                device_id_type=MESH,
            ).start()
        return carry

    lax.fori_loop(1, 64, ask, 0)
    pltpu.make_async_remote_copy(
        src_ref=req.at[1 - mc],
        dst_ref=reqin.at[mc],
        send_sem=sem_req_s,
        recv_sem=sem_req_r.at[0],
        device_id=(gx, mx * 2 + 1 - mc),
        device_id_type=MESH,
    ).start()
    pltpu.make_async_copy(req.at[mc], reqin.at[mc], sem_req_r.at[0]).start()

    load(cx_ref, NX, cxs, 0, 2)
    load(cy_ref, NX, cys, 0, 3)
    load(cz_ref, NX, czs, 0, 4)
    load(pcx_ref, PXN, pcxs, 0, 5)
    load(pcy_ref, PXN, pcys, 0, 6)

    lev = lax.broadcasted_iota(jnp.int32, (LEV, 128), 0)
    lane = lax.broadcasted_iota(jnp.int32, (LEV, 128), 1)

    def edge_copies(field, count, packed, landing, at):
        def face(x):
            return field.at[x, pl.ds(8, LEV)] if count == NX else field.at[x]

        west = (gx > 0, face(1), face(count + 1), (gx - 1, gy))
        east = (gx < 15, face(count), face(0), (gx + 1, gy))
        south = (gy > 0, packed.at[0], landing.at[1], (gx, gy - 1))
        north = (gy < 7, packed.at[1], landing.at[0], (gx, gy + 1))
        made = []
        for k, (has, src, dst, target) in enumerate((west, east, south, north)):
            made.append(
                (
                    has,
                    pltpu.make_async_remote_copy(
                        src_ref=src,
                        dst_ref=dst,
                        send_sem=hs.at[at, k],
                        recv_sem=hr.at[at, k],
                        device_id=target,
                        device_id_type=MESH,
                    ),
                )
            )
        return made

    def edges_start(made):
        for has, copy in made:
            pl.when(has)(copy.start)

    def edges_wait(made):
        for k, other in ((0, 1), (1, 0), (2, 3), (3, 2)):
            pl.when(made[other][0])(made[k][1].wait_recv)

    def edges_sent(made):
        for has, copy in made:
            pl.when(has)(copy.wait_send)

    def clear_edges(field, count, landing):
        zero = jnp.zeros((LEV, 128), F32)

        @pl.when(gx == 0)
        def _():
            field[0, pl.ds(8 if count == NX else 0, LEV), :] = zero

        @pl.when(gx == 15)
        def _():
            field[count + 1, pl.ds(8 if count == NX else 0, LEV), :] = zero

        @pl.when(gy == 0)
        def _():
            landing[0] = zero

        @pl.when(gy == 7)
        def _():
            landing[1] = zero

    def pack_edges(field, count, packed):
        base = 8 if count == NX else 0

        def one(x, carry):
            low, high = carry
            here = field[x + 1, pl.ds(base, LEV), :]
            low = jnp.where(lane == x, pltpu.roll(here, x, 1), low)
            high = jnp.where(lane == x, pltpu.roll(here, x + 1, 1), high)
            return low, high

        zero = jnp.zeros((LEV, 128), F32)
        low, high = lax.fori_loop(0, count, one, (zero, zero), unroll=4)
        packed[0] = low
        packed[1] = high

    deep = 32
    lanec = lax.broadcasted_iota(jnp.int32, (deep, 128), 1)
    levc = lax.broadcasted_iota(jnp.int32, (deep, 128), 0)

    def across(field, base, x, l0, landing, cx, cy):
        rows = pl.ds(base + l0, deep)
        here = field[x + 1, rows, :]
        west, east = field[x, rows, :], field[x + 2, rows, :]
        edge = pl.ds(l0, deep)
        south = jnp.where(
            lanec == 0,
            pltpu.roll(landing[0, edge, :], lax.rem(128 - x, 128), 1),
            pltpu.roll(here, 1, 1),
        )
        north = jnp.where(
            lanec == 127, pltpu.roll(landing[1, edge, :], 127 - x, 1), pltpu.roll(here, 127, 1)
        )
        return here, here - cx * jnp.where(cx > 0, here - west, east - here) - cy * jnp.where(
            cy > 0, here - south, north - here
        )

    def advance(field, x, l0, landing):
        edge = pl.ds(l0, deep)
        here, adv = across(field, 8, x, l0, landing, cxs[x, edge, :], cys[x, edge, :])
        cz = czs[x, edge, :]
        lower, upper = field[x + 1, pl.ds(7 + l0, deep), :], field[x + 1, pl.ds(9 + l0, deep), :]
        below = jnp.where(levc + (l0 - 1) >= terrain_ref[pl.ds(x, 1), :], lower, here)
        above = jnp.where(levc == LEV - 1 - l0, here, upper)
        return adv - cz * jnp.where(cz > 0, here - below, above - here)

    clear_edges(pq, PXN, pys)
    clear_edges(q0, NX, ybuf.at[0])
    clear_edges(q1, NX, ybuf.at[1])
    clear_edges(q2, NX, ybuf.at[2])

    blank8 = jnp.zeros((8, 128), F32)
    loaded(nraw, 0, NX, 1)

    def start_nest(x, carry):
        for field in (q0, q1, q2):
            field[x + 1, 0:8, :] = blank8
            field[x + 1, LEV + 8 : LEV + 16, :] = blank8
        q0[x + 1, 8 : LEV + 8, :] = jnp.where(lev >= terrain_ref[pl.ds(x, 1), :], nraw[x], 0.0)
        return carry

    lax.fori_loop(0, NX, start_nest, 0)
    pack_edges(q0, NX, ypack.at[0])
    q0_edges = edge_copies(q0, NX, ypack.at[0], ybuf.at[0], 0)
    edges_start(q0_edges)

    loaded(pq, 1, PXN, 0)

    def split(x, carry):
        shi[x], slo[x] = halves(pq[x + 1])
        return carry

    lax.fori_loop(0, PXN, split, 0, unroll=2)
    shi[PXN] = jnp.zeros((LEV, 128), BF16)
    slo[PXN] = jnp.zeros((LEV, 128), BF16)
    pack_edges(pq, PXN, pyk)
    p_edges = edge_copies(pq, PXN, pyk, pys, 1)
    edges_start(p_edges)


    def asked(g):
        part = reqin.at[pl.ds(g * (128 // GROUPS), 128 // GROUPS)]
        pltpu.make_async_copy(part, part, sem_req_r.at[g]).wait()

    sub256 = lax.broadcasted_iota(jnp.int32, (256, 128), 0)
    left48 = lax.broadcasted_iota(jnp.int32, (48, 128), 1) < 64
    left4 = lax.broadcasted_iota(jnp.int32, (4, 128), 1) < 64

    def answer(n, tx, ty):
        a, b = reqin[2 * n], reqin[2 * n + 1]
        place = jnp.where(left4, a, pltpu.roll(b, 64, 1)).astype(jnp.int32)
        amount = jnp.where(left4, pltpu.roll(a, 64, 1), b)
        table = jnp.zeros((256, 128), F32)
        for j in range(4):
            table = jnp.where(sub256 == place[j : j + 1], amount[j : j + 1], table)
        right = jnp.concatenate(halves(table), axis=1)
        base = (tx * 8 + ty) * 2
        rows = []
        for core in range(2):
            first, second = slots_ref[base + 2 * core], slots_ref[base + 2 * core + 1]
            rows.append(jnp.concatenate([shi[first], shi[second]], axis=1))
            rows.append(jnp.concatenate([slo[first], slo[second]], axis=1))
        out = jnp.dot(jnp.concatenate(rows, axis=0), right, preferred_element_type=F32)
        v0 = out[0:96, :128] + out[0:96, 128:] + out[96:192, :128]
        v1 = out[192:288, :128] + out[192:288, 128:] + out[288:384, :128]
        return (
            jnp.where(left48, v0[:48], pltpu.roll(v0[48:], 64, 1)),
            jnp.where(left48, pltpu.roll(v1[:48], 64, 1), v1[48:]),
        )

    def reply(base, count):
        places = [chip(base + u, -1) for u in range(count)]
        made = [answer(base + u, *places[u]) for u in range(count)]
        for u in range(count):
            ans[2 * (base + u)], ans[2 * (base + u) + 1] = made[u]
        for u in range(count):
            n = base + u
            tx, ty = places[u]
            for core in range(2):
                pltpu.make_async_remote_copy(
                    src_ref=ans.at[2 * n + core],
                    dst_ref=ansin.at[2 * n + mc],
                    send_sem=sem_ans_s,
                    recv_sem=sem_ans_r.at[lax.div(n, 64 // GROUPS)],
                    device_id=(tx, ty + core),
                    device_id_type=MESH,
                ).start()

    def replies(r, carry):
        asked(r)
        reply(8 * r, 4)
        reply(8 * r + 4, 4)
        return carry

    asked(0)
    ans[0], ans[1] = answer(0, gx, mx * 2)
    pltpu.make_async_remote_copy(
        src_ref=ans.at[1 - mc],
        dst_ref=ansin.at[mc],
        send_sem=sem_ans_s,
        recv_sem=sem_ans_r.at[0],
        device_id=(gx, mx * 2 + 1 - mc),
        device_id_type=MESH,
    ).start()
    pltpu.make_async_copy(ans.at[mc], ansin.at[mc], sem_ans_r.at[0]).start()
    reply(jnp.int32(1), 3)
    reply(jnp.int32(4), 4)
    lax.fori_loop(1, GROUPS, replies, 0)

    for k, (target, count) in enumerate(
        ((cxs, NX), (cys, NX), (czs, NX), (pcxs, PXN), (pcys, PXN))
    ):
        loaded(target, 0, count, k + 2)
    edges_wait(q0_edges)
    chunks = range(0, LEV, deep)

    def first_nest(x, carry):
        for l0 in chunks:
            adv1[x, pl.ds(l0, deep), :] = advance(q0, x, l0, ybuf.at[0])
        bound[x] = jnp.zeros((LEV, 128), F32)
        return carry

    lax.fori_loop(0, NX, first_nest, 0)

    edges_wait(p_edges)
    sub512 = lax.broadcasted_iota(jnp.int32, (256, 512), 0)
    ones8 = jnp.ones((8, 512), BF16)

    def parents(i, carry):
        hot = jnp.where(sub512 == fbt_ref[...] - 256 * i, 1.0, 0.0).astype(BF16)
        tmat[i] = hot
        left = 1.0 - 0.5 * lax.dot_general(ones8, hot, NT, preferred_element_type=F32)[0:1]
        for k in range(2):
            x = 2 * i + k
            for l0 in chunks:
                edge = pl.ds(l0, deep)
                moved = across(pq, 0, x, l0, pys, pcxs[x, edge, :], pcys[x, edge, :])[1]
                keep[x, edge, :] = moved * left[:, 128 * k : 128 * k + 128]
        return carry

    lax.fori_loop(0, PXN // 2, parents, 0)

    sub16 = lax.broadcasted_iota(jnp.int32, (16, 128), 0)

    fbt[...] = jnp.full((128, 256), -1.0, F32)

    def turn(i, carry):
        fbt[pl.ds(i, 1), :] = fbi_ref[i].astype(F32)
        return carry

    lax.fori_loop(0, 81, turn, 0)
    fbn[...] = jnp.transpose(fbt[...]).astype(jnp.int32)

    def count(r, carry):
        made = []
        for u in range(8):
            highs, lows = [], []
            for k in range(2):
                row = fbn[pl.ds(16 * r + 2 * u + k, 1), :]
                high = jnp.where(sub16 == (row >> 7), 1.0, 0.0).astype(BF16)
                blank = jnp.zeros((16, 128), BF16)
                highs.append(jnp.concatenate([high, blank] if k == 0 else [blank, high], axis=1))
                lows.append(jnp.where(sub128 == (row & 127), 1.0, 0.0).astype(BF16))
            made.append(
                lax.dot_general(
                    jnp.concatenate(highs, axis=0),
                    jnp.concatenate(lows, axis=1),
                    NT,
                    preferred_element_type=F32,
                )
            )
        for u in range(8):
            counts[16 * r + 2 * u] = made[u][:16]
            counts[16 * r + 2 * u + 1] = made[u][16:]
        return carry

    lax.fori_loop(0, 16, count, 0)
    row256 = lax.broadcasted_iota(jnp.int32, (256, 512), 0)
    chosen = jnp.transpose(jnp.where(row256 == fbs_ref[...], 1.0, 0.0)).astype(BF16)
    for x in range(NX):
        cmat[:, 128 * x : 128 * x + 128] = jnp.dot(
            chosen, counts[:, x, :].astype(BF16), preferred_element_type=F32
        ).astype(BF16)
    qmat[...] = jnp.zeros_like(qmat)


    per = 64 // GROUPS
    for g in range(GROUPS):
        part = ansin.at[pl.ds(2 * per * g, 2 * per)]
        pltpu.make_async_copy(part, part, sem_ans_r.at[g]).wait()
        for i in range(per):
            a, b = ansin[2 * (per * g + i)], ansin[2 * (per * g + i) + 1]
            upper = jnp.where(left48, a, pltpu.roll(b, 64, 1))
            lower = jnp.where(left48, pltpu.roll(a, 64, 1), b)
            high, low = halves(jnp.concatenate([upper, lower], axis=0))
            xmat[0:96, 128 * i : 128 * i + 128] = high
            xmat[96:192, 128 * i : 128 * i + 128] = low

        def pick(x, carry, g=g):
            hots = []
            for k in range(2):
                owner = jnp.broadcast_to(relm[pl.ds(2 * x + k, 1), :], (16, 128))
                ranks = rankm[2 * x + k]
                blocks = []
                for i in range(2 * per):
                    mine = jnp.where(owner == 2 * per * g + i, 1.0, 0.0).astype(BF16)
                    blocks.append(ranks * jnp.concatenate([mine] * (KREQ // 16), axis=0))
                hots.append(jnp.concatenate(blocks, axis=0))
            got = jnp.dot(xmat[...], jnp.concatenate(hots, axis=1), preferred_element_type=F32)
            bound[2 * x] += got[:96, :128] + got[96:, :128]
            bound[2 * x + 1] += got[:96, 128:] + got[96:, 128:]
            return carry

        lax.fori_loop(0, NX // 2, pick, 0)

    def settle(x, l0, adv):
        terrain = terrain_ref[pl.ds(x, 1), :]
        rel = relax_ref[pl.ds(x, 1), :]
        pull = bound[x, pl.ds(l0, deep), :] - adv
        return jnp.where(levc + l0 >= terrain, adv + rel * pull, 0.0)

    def first_settle(x, carry):
        for l0 in chunks:
            q1[x + 1, pl.ds(8 + l0, deep), :] = settle(x, l0, adv1[x, pl.ds(l0, deep), :])
        return carry

    lax.fori_loop(0, NX, first_settle, 0)
    edges = [q0_edges, p_edges]

    def exchange(now, step):
        pack_edges(now, NX, ypack.at[step])
        made = edge_copies(now, NX, ypack.at[step], ybuf.at[step], step + 1)
        edges_start(made)
        edges_wait(made)
        edges.append(made)

    exchange(q1, 1)

    def second(x, carry):
        for l0 in chunks:
            q2[x + 1, pl.ds(8 + l0, deep), :] = settle(x, l0, advance(q1, x, l0, ybuf.at[1]))
        return carry

    lax.fori_loop(0, NX, second, 0)
    exchange(q2, 2)

    def third(x, carry):
        at = pl.ds(pl.multiple_of(128 * x, 128), 128)
        for l0 in chunks:
            value = settle(x, l0, advance(q2, x, l0, ybuf.at[2]))
            nres[x, pl.ds(l0, deep), :] = value
            high, low = halves(value)
            qmat[pl.ds(l0, deep), at] = high
            qmat[pl.ds(128 + l0, deep), at] = low
        return carry

    lax.fori_loop(0, NX, third, 0)

    got = lax.dot_general(cmat[...], qmat[...], NT, preferred_element_type=F32)
    rows = (got[:, :128] + got[:, 128:]) * (1.0 / 81.0)
    lane512 = lax.broadcasted_iota(jnp.int32, (512, 128), 1)
    rows = jnp.where(lane512 == LEV, flag, rows)
    fbsend[...] = rows.reshape(128, 4, 128)

    def feed(n, carry):
        tx, ty = chip(n, 1)
        for core in range(2):
            pltpu.make_async_remote_copy(
                src_ref=fbsend.at[tx * 8 + ty + core],
                dst_ref=fbin.at[me],
                send_sem=sem_fb_s,
                recv_sem=sem_fb_r,
                device_id=(tx, ty + core),
                device_id_type=MESH,
            ).start()
        return carry

    lax.fori_loop(1, 64, feed, 0)
    other = mx * 2 + 1 - mc
    pltpu.make_async_remote_copy(
        src_ref=fbsend.at[gx * 8 + other],
        dst_ref=fbin.at[me],
        send_sem=sem_fb_s,
        recv_sem=sem_fb_r,
        device_id=(gx, other),
        device_id_type=MESH,
    ).start()
    pltpu.make_async_copy(fbsend.at[me], fbin.at[me], sem_fb_r).start()

    def store_nest(x, carry):
        pltpu.make_async_copy(nres.at[x], nest_out.at[:, x], sem_out.at[0]).start()
        return carry

    lax.fori_loop(0, NX, store_nest, 0)
    pltpu.make_async_copy(fbin, fbin, sem_fb_r).wait()


    values = fbin[...].reshape(512, 128)
    high, low = halves(jnp.transpose(values)[:96])
    both = jnp.concatenate([high, low], axis=0)
    for i in range(PXN // 2):
        got = lax.dot_general(both, tmat[i], NT, preferred_element_type=F32)
        for k in range(2):
            x, at = 2 * i + k, slice(128 * k, 128 * k + 128)
            keep[x] += 0.5 * (got[:96, at] + got[96:, at])
            pltpu.make_async_copy(keep.at[x], parent_out.at[:, x], sem_out.at[1]).start()
    worst = jnp.max(jnp.where(lane512 == LEV, values, 0.0))
    flag_out[0] = jnp.where(worst > 0.5, 1, 0)
    pltpu.make_async_copy(nres, nres, sem_out.at[0]).wait()
    pltpu.make_async_copy(keep, keep, sem_out.at[1]).wait()

    for buffer, sem in ((req, sem_req_s), (ans, sem_ans_s), (fbsend, sem_fb_s)):
        part = buffer.at[pl.ds(0, 127)]
        pltpu.make_async_copy(part, part, sem).wait()
    for made in edges:
        edges_sent(made)


def fused_step(
    nest_field,
    courant_x,
    courant_y,
    courant_z,
    terrain,
    relax,
    interp_index,
    interp_weight,
    send_slots,
    parent_field,
    parent_cx,
    parent_cy,
    fb_index,
    fb_slot,
    fb_target,
):
    vmem = pl.BlockSpec(memory_space=pltpu.VMEM)
    smem = pl.BlockSpec(memory_space=pltpu.SMEM)
    hbm = pl.BlockSpec(memory_space=pl.ANY)
    slab = (LEV, 128)
    scratch = [
        pltpu.VMEM((NX + 2, LEV + 16, 128), F32),
        pltpu.VMEM((NX + 2, LEV + 16, 128), F32),
        pltpu.VMEM((NX + 2, LEV + 16, 128), F32),
        pltpu.VMEM((3, 2) + slab, F32),
        pltpu.VMEM((3, 2) + slab, F32),
        pltpu.VMEM((NX,) + slab, F32),
        pltpu.VMEM((NX,) + slab, F32),
        pltpu.VMEM((PXN + 2,) + slab, F32),
        pltpu.VMEM((2,) + slab, F32),
        pltpu.VMEM((2,) + slab, F32),
        pltpu.VMEM((PXN,) + slab, F32),
        pltpu.VMEM((PXN + 1,) + slab, BF16),
        pltpu.VMEM((PXN + 1,) + slab, BF16),
        pltpu.VMEM((128, 4, 128), F32),
        pltpu.VMEM((128, 4, 128), F32),
        pltpu.VMEM((128, 48, 128), F32),
        pltpu.VMEM((128, 48, 128), F32),
        pltpu.VMEM((192, 64 // GROUPS * 128), BF16),
        pltpu.VMEM((256, NX, 128), F32),
        pltpu.VMEM((512, NX * 128), BF16),
        pltpu.VMEM((256, NX * 128), BF16),
        pltpu.VMEM((PXN // 2, 256, 512), BF16),
        pltpu.VMEM((128, 4, 128), F32),
        pltpu.VMEM((128, 4, 128), F32),
        pltpu.VMEM((128, NX * 128), BF16),
        pltpu.VMEM((1024, NX * 128), BF16),
        pltpu.VMEM((NX, KREQ, 128), BF16),
        pltpu.VMEM((NX, 128), jnp.int32),
        pltpu.VMEM((NX,) + slab, F32),
        pltpu.VMEM((NX,) + slab, F32),
        pltpu.VMEM((NX,) + slab, F32),
        pltpu.VMEM((NX,) + slab, F32),
        pltpu.VMEM((PXN,) + slab, F32),
        pltpu.VMEM((PXN,) + slab, F32),
        pltpu.VMEM((NX,) + slab, F32),
        pltpu.VMEM((128, 256), F32),
        pltpu.VMEM((256, 128), jnp.int32),
        pltpu.SemaphoreType.DMA((7,)),
        pltpu.SemaphoreType.DMA((2,)),
        pltpu.SemaphoreType.DMA,
        pltpu.SemaphoreType.DMA((GROUPS,)),
        pltpu.SemaphoreType.DMA,
        pltpu.SemaphoreType.DMA((GROUPS,)),
        pltpu.SemaphoreType.DMA,
        pltpu.SemaphoreType.DMA,
        pltpu.SemaphoreType.DMA((4, 4)),
        pltpu.SemaphoreType.DMA((4, 4)),
    ]
    return pl.pallas_call(
        step_kernel,
        out_shape=(
            jax.ShapeDtypeStruct(nest_field.shape, F32),
            jax.ShapeDtypeStruct(parent_field.shape, F32),
            jax.ShapeDtypeStruct((1,), jnp.int32),
        ),
        in_specs=[smem] + [hbm] * 4 + [vmem] * 4 + [hbm] * 3 + [vmem] * 3,
        out_specs=(hbm, hbm, smem),
        scratch_shapes=scratch,
        compiler_params=pltpu.CompilerParams(
            collective_id=0, has_side_effects=True, vmem_limit_bytes=56 * 2**20
        ),
        name="step",
    )(
        send_slots[0],
        nest_field,
        courant_x,
        courant_y,
        courant_z,
        terrain,
        relax,
        interp_index,
        interp_weight,
        parent_field,
        parent_cx,
        parent_cy,
        jnp.transpose(fb_index, (2, 0, 1)),
        fb_slot,
        fb_target,
    )


def on_device(*args):
    nest_out, parent_out, flags = fused_step(*args)
    return lax.cond(
        flags[0] > 0, lambda: dense_step(*args), lambda: (nest_out, parent_out)
    )


def solution(mesh):
    in_specs = (
        P(None, "gx", "gy"),
        P(None, "gx", "gy"),
        P(None, "gx", "gy"),
        P(None, "gx", "gy"),
        P("gx", "gy"),
        P("gx", "gy"),
        P(None, "gx", "gy"),
        P(None, "gx", "gy"),
        P(("gx", "gy"), None),
        P(None, "gx", "gy"),
        P(None, "gx", "gy"),
        P(None, "gx", "gy"),
        P(("gx", "gy"), None, None),
        P(("gx", "gy"), None),
        P(("gx", "gy"), None),
    )
    out_specs = (P(None, "gx", "gy"), P(None, "gx", "gy"))
    return jax.shard_map(
        on_device, mesh=mesh, in_specs=in_specs, out_specs=out_specs, check_vma=False
    )
```

profile of v0, /device:TPU:1, one launch (start us, length us, event | category | flops | bytes accessed | tf_op | source)
XLA Modules:
  0.0 97.2 jit_solution(712486408973438591)
XLA Ops:
  0.6 0.0 copy-start.6
  0.6 0.0 copy-start.10
  0.7 0.0 copy-start.15
  0.7 0.0 copy-start.16
  0.7 0.0 copy-start.17
  0.7 0.0 copy-start.18
  0.7 0.0 copy-start.19
  0.7 0.0 copy-start.24
  0.7 0.0 copy-start.25
  0.7 0.0 copy-start.27
  0.7 92.2 %step.1 = (f32[96,16,128]{2,1,0:T(8,128)}, f32[96,32,128]{2,1,0:T(8,128)}, s32[1]{0:T(128)}) custom-call(s32[256]{0:T(256)} %bitcast.82, f32[96,16,128]{2,1,0:T(8,128)} %nest_ref.1, f32[96,16,128]{2,1,0:T(8,128)} %cx_ref.1, f32[96,16,128]{2,1,0:T(8,128)} %cy_ref.1, f32[96,16,128]{2,1,0:T(8,128)} %cz_ref.1, s32[16,128]{1,0:T(8,128)} %terrain_ref.1, ...), custom_call_target="tpu_custom_call" | custom-call | tf_op jit(solution)/shard_map/step/pallas_call | solution.py:801
  93.6 0.0 copy-done.6
  93.6 0.0 copy-done.10
  93.6 0.0 copy-done.15
  93.6 0.0 copy-done.16
  93.6 0.0 copy-done.17
  93.6 0.0 copy-done.18
  93.6 0.0 copy-done.19
  93.6 0.0 copy-done.24
  93.7 0.0 copy-done.25
  93.7 0.0 copy-done.27
  93.7 0.2 conditional.1
  93.9 0.0 copy-start.14
  93.9 2.2 %copy.74 = f32[96,16,128]{2,1,0:T(8,128)} copy(f32[96,16,128]{2,1,0:T(8,128)} %get-tuple-element.170) | data formatting | bytes 1572864
  96.1 0.0 copy-done.14
  96.1 1.1 %copy.75 = f32[96,32,128]{2,1,0:T(8,128)} copy(f32[96,32,128]{2,1,0:T(8,128)S(1)} %copy-done.14) | data formatting | bytes 3145728
Async XLA Ops:
  0.6 92.9 %copy-start.6 = (f32[96,32,128]{2,1,0:T(8,128)S(1)}, f32[96,32,128]{2,1,0:T(8,128)}, u32[]{:S(2)}) copy-start(f32[96,32,128]{2,1,0:T(8,128)} %parent_ref.1) | copy-start | bytes 4718596
  0.6 92.9 %copy-start.10 = (f32[96,16,128]{2,1,0:T(8,128)S(1)}, f32[96,16,128]{2,1,0:T(8,128)}, u32[]{:S(2)}) copy-start(f32[96,16,128]{2,1,0:T(8,128)} %nest_ref.1) | copy-start | bytes 2359300
  0.7 92.9 %copy-start.15 = (s32[1,256,81]{1,0,2:T(1,128)S(1)}, s32[1,256,81]{1,0,2:T(1,128)}, u32[]{:S(2)}) copy-start(s32[1,256,81]{1,0,2:T(1,128)} %param.31) | copy-start | bytes 248836
  0.7 92.9 %copy-start.16 = (s32[4,16,128]{2,1,0:T(8,128)S(1)}, s32[4,16,128]{2,1,0:T(8,128)}, u32[]{:S(2)}) copy-start(s32[4,16,128]{2,1,0:T(8,128)} %index_ref.1) | copy-start | bytes 98308
  0.7 92.9 %copy-start.17 = (s32[16,128]{1,0:T(8,128)S(1)}, s32[16,128]{1,0:T(8,128)}, u32[]{:S(2)}) copy-start(s32[16,128]{1,0:T(8,128)} %terrain_ref.1) | copy-start | bytes 24580
  0.7 92.9 %copy-start.18 = (f32[4,16,128]{2,1,0:T(8,128)S(1)}, f32[4,16,128]{2,1,0:T(8,128)}, u32[]{:S(2)}) copy-start(f32[4,16,128]{2,1,0:T(8,128)} %weight_ref.1) | copy-start | bytes 98308
  0.7 92.9 %copy-start.19 = (f32[16,128]{1,0:T(8,128)S(1)}, f32[16,128]{1,0:T(8,128)}, u32[]{:S(2)}) copy-start(f32[16,128]{1,0:T(8,128)} %relax_ref.1) | copy-start | bytes 24580
  0.7 92.9 %copy-start.24 = (s32[1,512]{1,0:T(1,128)S(1)}, s32[1,512]{1,0:T(1,128)}, u32[]{:S(2)}) copy-start(s32[1,512]{1,0:T(1,128)} %fbs_ref.1) | copy-start | bytes 6148
  0.7 92.9 %copy-start.25 = (s32[1,512]{1,0:T(1,128)S(1)}, s32[1,512]{1,0:T(1,128)}, u32[]{:S(2)}) copy-start(s32[1,512]{1,0:T(1,128)} %fbt_ref.1) | copy-start | bytes 6148
  0.7 92.9 %copy-start.27 = (s32[1,256]{1,0:T(1,128)S(1)}, s32[1,256]{1,0:T(1,128)}, u32[]{:S(2)}) copy-start(s32[1,256]{1,0:T(1,128)} %param.27) | copy-start | bytes 3076
  93.9 2.2 %copy-start.14 = (f32[96,32,128]{2,1,0:T(8,128)S(1)}, f32[96,32,128]{2,1,0:T(8,128)}, u32[]{:S(2)}) copy-start(f32[96,32,128]{2,1,0:T(8,128)} %get-tuple-element.171) | copy-start | bytes 4718596
where the time goes:
time: 97.4 us; the launch traced here: 97.2 us
  Pallas kernels  92.2 us (95%)
  local copies, waits for them, and re-layouts  3.37 us (3%)
  between operations  1.45 us (1%)
    pallas_call x1, Pallas kernels, fused_step(): pl.pallas_call(step_kernel, out_shape=(jax.ShapeDtypeStruct(nest_field.sh...  92.2 us
    unnamed x24, local copies, waits for them, and re-layouts  3.37 us

commit v1 on v0

--- a/solution.py
+++ b/solution.py
@@ -382,7 +382,7 @@
             return low, high
 
         zero = jnp.zeros((LEV, 128), F32)
-        low, high = lax.fori_loop(0, count, one, (zero, zero), unroll=4)
+        low, high = lax.fori_loop(0, count, one, (zero, zero), unroll=16)
         packed[0] = low
         packed[1] = high
 
@@ -623,7 +623,7 @@
             bound[2 * x + 1] += got[:96, 128:] + got[96:, 128:]
             return carry
 
-        lax.fori_loop(0, NX // 2, pick, 0)
+        lax.fori_loop(0, NX // 2, pick, 0, unroll=2)
 
     def settle(x, l0, adv):
         terrain = terrain_ref[pl.ds(x, 1), :]
@@ -653,7 +653,7 @@
             q2[x + 1, pl.ds(8 + l0, deep), :] = settle(x, l0, advance(q1, x, l0, ybuf.at[1]))
         return carry
 
-    lax.fori_loop(0, NX, second, 0)
+    lax.fori_loop(0, NX, second, 0, unroll=4)
     exchange(q2, 2)
 
     def third(x, carry):
@@ -666,7 +666,7 @@
             qmat[pl.ds(128 + l0, deep), at] = low
         return carry
 
-    lax.fori_loop(0, NX, third, 0)
+    lax.fori_loop(0, NX, third, 0, unroll=4)
 
     got = lax.dot_general(cmat[...], qmat[...], NT, preferred_element_type=F32)
     rows = (got[:, :128] + got[:, 128:]) * (1.0 / 81.0)
@@ -831,10 +831,39 @@
     )
 
 
+def hand_over(nest_ref, parent_ref, nest_out, parent_out, sem):
+    copies = []
+    for k, (source, target) in enumerate(((nest_ref, nest_out), (parent_ref, parent_out))):
+        for part in range(8):
+            rows = pl.ds(12 * part, 12)
+            copies.append(
+                pltpu.make_async_copy(source.at[rows], target.at[rows], sem.at[k, part])
+            )
+    for copy in copies:
+        copy.start()
+    for copy in copies:
+        copy.wait()
+
+
+def handed(nest_out, parent_out):
+    hbm = pl.BlockSpec(memory_space=pl.ANY)
+    return pl.pallas_call(
+        hand_over,
+        out_shape=(
+            jax.ShapeDtypeStruct(nest_out.shape, F32),
+            jax.ShapeDtypeStruct(parent_out.shape, F32),
+        ),
+        in_specs=[hbm, hbm],
+        out_specs=(hbm, hbm),
+        scratch_shapes=[pltpu.SemaphoreType.DMA((2, 8))],
+        name="hand_over",
+    )(nest_out, parent_out)
+
+
 def on_device(*args):
     nest_out, parent_out, flags = fused_step(*args)
     return lax.cond(
-        flags[0] > 0, lambda: dense_step(*args), lambda: (nest_out, parent_out)
+        flags[0] > 0, lambda: dense_step(*args), lambda: handed(nest_out, parent_out)
     )
 
 

time: 97.4 us -> 161 us (1.65)
  Pallas kernels: 92.2 us -> 159 us
  local copies, waits for them, and re-layouts: 3.37 us -> 0.04 us
    pallas_call x0 -> x1, Pallas kernels: none -> 72.7 us  [handed(): pl.pallas_call(hand_over, out_shape=(jax.ShapeDtypeStruct(nest_out.shape,...]
    pallas_call x1, Pallas kernels: 92.2 us -> 85.8 us  [fused_step(): pl.pallas_call(step_kernel, out_shape=(jax.ShapeDtypeStruct(nest_field.sh...]
    unnamed x24 -> x20, local copies, waits for them, and re-layouts: 3.37 us -> 0.04 us
where the time goes in v1:
time: 161 us; the launch traced here: 160 us
  Pallas kernels  159 us (99%)
    pallas_call x1, Pallas kernels, fused_step(): pl.pallas_call(step_kernel, out_shape=(jax.ShapeDtypeStruct(nest_field.sh...  85.8 us
    pallas_call x1, Pallas kernels, handed(): pl.pallas_call(hand_over, out_shape=(jax.ShapeDtypeStruct(nest_out.shape,...  72.7 us

profile of v1, /device:TPU:1, one launch (start us, length us, event | category | flops | bytes accessed | tf_op | source)
XLA Modules:
  0.0 160.4 jit_solution(879140028842955903)
XLA Ops:
  0.6 0.0 copy-start.6
  0.6 0.0 copy-start.10
  0.7 0.0 copy-start.14
  0.7 0.0 copy-start.15
  0.7 0.0 copy-start.16
  0.7 0.0 copy-start.17
  0.7 0.0 copy-start.18
  0.7 0.0 copy-start.23
  0.7 0.0 copy-start.24
  0.7 0.0 copy-start.26
  0.7 85.8 %step.1 = (f32[96,16,128]{2,1,0:T(8,128)}, f32[96,32,128]{2,1,0:T(8,128)}, s32[1]{0:T(128)}) custom-call(s32[256]{0:T(256)} %bitcast.82, f32[96,16,128]{2,1,0:T(8,128)} %nest_ref.1, f32[96,16,128]{2,1,0:T(8,128)} %cx_ref.1, f32[96,16,128]{2,1,0:T(8,128)} %cy_ref.1, f32[96,16,128]{2,1,0:T(8,128)} %cz_ref.1, s32[16,128]{1,0:T(8,128)} %terrain_ref.1, ...), custom_call_target="tpu_custom_call" | custom-call | tf_op jit(solution)/shard_map/step/pallas_call | solution.py:801
  87.1 0.0 copy-done.6
  87.1 0.0 copy-done.10
  87.2 0.0 copy-done.14
  87.2 0.0 copy-done.15
  87.2 0.0 copy-done.16
  87.2 0.0 copy-done.17
  87.2 0.0 copy-done.18
  87.2 0.0 copy-done.23
  87.2 0.0 copy-done.24
  87.2 0.0 copy-done.26
  87.2 73.0 %conditional.1 = ((f32[96,16,128]{2,1,0:T(8,128)}, f32[96,32,128]{2,1,0:T(8,128)})) conditional(s32[]{:T(128)} %bitcast.31, (f32[96,16,128]{2,1,0:T(8,128)}, f32[96,32,128]{2,1,0:T(8,128)}) %tuple.15, (s32[16,128]{1,0:T(8,128)S(1)}, f32[96,16,128]{2,1,0:T(8,128)S(1)}, f32[96,16,128]{2,1,0:T(8,128)}, f32[96,16,128]{2,1,0:T(8,128)}, ...), branch_computations={%region_0.0_spmd, %region_1.5_spmd} | conditional | flops 1243548160 | bytes 294960576 | solution.py:865
  87.2 72.7 %hand_over.1 = (f32[96,16,128]{2,1,0:T(8,128)}, f32[96,32,128]{2,1,0:T(8,128)}) custom-call(f32[96,16,128]{2,1,0:T(8,128)} %get-tuple-element.18.nest_ref, f32[96,32,128]{2,1,0:T(8,128)} %get-tuple-element.36.parent_ref), custom_call_target="tpu_custom_call" | custom-call | tf_op jit(solution)/shard_map/cond/branch_0_fun/hand_over/pallas_call | solution.py:850
Async XLA Ops:
  0.6 86.5 %copy-start.6 = (f32[96,32,128]{2,1,0:T(8,128)S(1)}, f32[96,32,128]{2,1,0:T(8,128)}, u32[]{:S(2)}) copy-start(f32[96,32,128]{2,1,0:T(8,128)} %parent_ref.1) | copy-start | bytes 4718596
  0.6 86.5 %copy-start.10 = (f32[96,16,128]{2,1,0:T(8,128)S(1)}, f32[96,16,128]{2,1,0:T(8,128)}, u32[]{:S(2)}) copy-start(f32[96,16,128]{2,1,0:T(8,128)} %nest_ref.1) | copy-start | bytes 2359300
  0.7 86.5 %copy-start.14 = (s32[1,256,81]{1,0,2:T(1,128)S(1)}, s32[1,256,81]{1,0,2:T(1,128)}, u32[]{:S(2)}) copy-start(s32[1,256,81]{1,0,2:T(1,128)} %param.31) | copy-start | bytes 248836
  0.7 86.5 %copy-start.15 = (s32[4,16,128]{2,1,0:T(8,128)S(1)}, s32[4,16,128]{2,1,0:T(8,128)}, u32[]{:S(2)}) copy-start(s32[4,16,128]{2,1,0:T(8,128)} %index_ref.1) | copy-start | bytes 98308
  0.7 86.5 %copy-start.16 = (s32[16,128]{1,0:T(8,128)S(1)}, s32[16,128]{1,0:T(8,128)}, u32[]{:S(2)}) copy-start(s32[16,128]{1,0:T(8,128)} %terrain_ref.1) | copy-start | bytes 24580
  0.7 86.5 %copy-start.17 = (f32[4,16,128]{2,1,0:T(8,128)S(1)}, f32[4,16,128]{2,1,0:T(8,128)}, u32[]{:S(2)}) copy-start(f32[4,16,128]{2,1,0:T(8,128)} %weight_ref.1) | copy-start | bytes 98308
  0.7 86.5 %copy-start.18 = (f32[16,128]{1,0:T(8,128)S(1)}, f32[16,128]{1,0:T(8,128)}, u32[]{:S(2)}) copy-start(f32[16,128]{1,0:T(8,128)} %relax_ref.1) | copy-start | bytes 24580
  0.7 86.5 %copy-start.23 = (s32[1,512]{1,0:T(1,128)S(1)}, s32[1,512]{1,0:T(1,128)}, u32[]{:S(2)}) copy-start(s32[1,512]{1,0:T(1,128)} %fbs_ref.1) | copy-start | bytes 6148
  0.7 86.5 %copy-start.24 = (s32[1,512]{1,0:T(1,128)S(1)}, s32[1,512]{1,0:T(1,128)}, u32[]{:S(2)}) copy-start(s32[1,512]{1,0:T(1,128)} %fbt_ref.1) | copy-start | bytes 6148
  0.7 86.5 %copy-start.26 = (s32[1,256]{1,0:T(1,128)S(1)}, s32[1,256]{1,0:T(1,128)}, u32[]{:S(2)}) copy-start(s32[1,256]{1,0:T(1,128)} %param.27) | copy-start | bytes 3076

commit v2 on v1

--- a/solution.py
+++ b/solution.py
@@ -306,11 +306,6 @@
     ).start()
     pltpu.make_async_copy(req.at[mc], reqin.at[mc], sem_req_r.at[0]).start()
 
-    load(cx_ref, NX, cxs, 0, 2)
-    load(cy_ref, NX, cys, 0, 3)
-    load(cz_ref, NX, czs, 0, 4)
-    load(pcx_ref, PXN, pcxs, 0, 5)
-    load(pcy_ref, PXN, pcys, 0, 6)
 
     lev = lax.broadcasted_iota(jnp.int32, (LEV, 128), 0)
     lane = lax.broadcasted_iota(jnp.int32, (LEV, 128), 1)
@@ -518,6 +513,11 @@
     reply(jnp.int32(1), 3)
     reply(jnp.int32(4), 4)
     lax.fori_loop(1, GROUPS, replies, 0)
+    load(cx_ref, NX, cxs, 0, 2)
+    load(cy_ref, NX, cys, 0, 3)
+    load(cz_ref, NX, czs, 0, 4)
+    load(pcx_ref, PXN, pcxs, 0, 5)
+    load(pcy_ref, PXN, pcys, 0, 6)
 
     for k, (target, count) in enumerate(
         ((cxs, NX), (cys, NX), (czs, NX), (pcxs, PXN), (pcys, PXN))
@@ -623,7 +623,7 @@
             bound[2 * x + 1] += got[:96, 128:] + got[96:, 128:]
             return carry
 
-        lax.fori_loop(0, NX // 2, pick, 0, unroll=2)
+        lax.fori_loop(0, NX // 2, pick, 0, unroll=4)
 
     def settle(x, l0, adv):
         terrain = terrain_ref[pl.ds(x, 1), :]
@@ -831,17 +831,23 @@
     )
 
 
-def hand_over(nest_ref, parent_ref, nest_out, parent_out, sem):
-    copies = []
-    for k, (source, target) in enumerate(((nest_ref, nest_out), (parent_ref, parent_out))):
-        for part in range(8):
-            rows = pl.ds(12 * part, 12)
-            copies.append(
-                pltpu.make_async_copy(source.at[rows], target.at[rows], sem.at[k, part])
+def hand_over(nest_ref, parent_ref, nest_out, parent_out, nest_buf, parent_buf, come, go):
+    arriving, leaving = [], []
+    for part in range(4):
+        rows = pl.ds(24 * part, 24)
+        for k, (source, held, target) in enumerate(
+            ((nest_ref, nest_buf, nest_out), (parent_ref, parent_buf, parent_out))
+        ):
+            arriving.append(
+                pltpu.make_async_copy(source.at[rows], held.at[rows], come.at[k, part])
             )
-    for copy in copies:
+            leaving.append(pltpu.make_async_copy(held.at[rows], target.at[rows], go.at[k, part]))
+    for copy in arriving:
         copy.start()
-    for copy in copies:
+    for first, second in zip(arriving, leaving):
+        first.wait()
+        second.start()
+    for copy in leaving:
         copy.wait()
 
 
@@ -855,7 +861,13 @@
         ),
         in_specs=[hbm, hbm],
         out_specs=(hbm, hbm),
-        scratch_shapes=[pltpu.SemaphoreType.DMA((2, 8))],
+        scratch_shapes=[
+            pltpu.VMEM(nest_out.shape, F32),
+            pltpu.VMEM(parent_out.shape, F32),
+            pltpu.SemaphoreType.DMA((2, 4)),
+            pltpu.SemaphoreType.DMA((2, 4)),
+        ],
+        compiler_params=pltpu.CompilerParams(vmem_limit_bytes=16 * 2**20),
         name="hand_over",
     )(nest_out, parent_out)
 

time: 161 us -> 93.5 us (0.58)
  Pallas kernels: 159 us -> 91.3 us
    pallas_call x1, Pallas kernels: 72.7 us -> 3.29 us  [handed(): pl.pallas_call(hand_over, out_shape=(jax.ShapeDtypeStruct(nest_out.shape,...]
    pallas_call x1, Pallas kernels: 85.8 us -> 88 us  [fused_step(): pl.pallas_call(step_kernel, out_shape=(jax.ShapeDtypeStruct(nest_field.sh...]
where the time goes in v2:
time: 93.5 us; the launch traced here: 93.3 us
  Pallas kernels  91.3 us (98%)
  between operations  1.67 us (2%)
    pallas_call x1, Pallas kernels, fused_step(): pl.pallas_call(step_kernel, out_shape=(jax.ShapeDtypeStruct(nest_field.sh...  88 us
    pallas_call x1, Pallas kernels, handed(): pl.pallas_call(hand_over, out_shape=(jax.ShapeDtypeStruct(nest_out.shape,...  3.29 us

profile of v2, /device:TPU:1, one launch (start us, length us, event | category | flops | bytes accessed | tf_op | source)
XLA Modules:
  0.0 93.3 jit_solution(2194167698621412969)
XLA Ops:
  0.6 0.0 copy-start.6
  0.6 0.0 copy-start.10
  0.7 0.0 copy-start.14
  0.7 0.0 copy-start.15
  0.7 0.0 copy-start.16
  0.7 0.0 copy-start.17
  0.7 0.0 copy-start.18
  0.7 0.0 copy-start.23
  0.7 0.0 copy-start.24
  0.7 0.0 copy-start.26
  0.7 88.0 %step.1 = (f32[96,16,128]{2,1,0:T(8,128)S(1)}, f32[96,32,128]{2,1,0:T(8,128)S(1)}, s32[1]{0:T(128)}) custom-call(s32[256]{0:T(256)} %bitcast.82, f32[96,16,128]{2,1,0:T(8,128)} %nest_ref.1, f32[96,16,128]{2,1,0:T(8,128)} %cx_ref.1, f32[96,16,128]{2,1,0:T(8,128)} %cy_ref.1, f32[96,16,128]{2,1,0:T(8,128)} %cz_ref.1, s32[16,128]{1,0:T(8,128)} %terrain_ref.1, ...), custom_call_target="tpu_custom_call" | custom-call | tf_op jit(solution)/shard_map/step/pallas_call | solution.py:801
  89.4 0.0 copy-done.6
  89.5 0.0 copy-done.10
  89.5 0.0 copy-done.14
  89.5 0.0 copy-done.15
  89.5 0.0 copy-done.16
  89.5 0.0 copy-done.17
  89.5 0.0 copy-done.18
  89.5 0.0 copy-done.23
  89.5 0.0 copy-done.24
  89.5 0.0 copy-done.26
  89.5 3.6 %conditional.1 = ((f32[96,16,128]{2,1,0:T(8,128)}, f32[96,32,128]{2,1,0:T(8,128)})) conditional(s32[]{:T(128)} %bitcast.31, (f32[96,16,128]{2,1,0:T(8,128)S(1)}, f32[96,32,128]{2,1,0:T(8,128)S(1)}) %tuple.15, (s32[16,128]{1,0:T(8,128)S(1)}, f32[96,16,128]{2,1,0:T(8,128)S(1)}, f32[96,16,128]{2,1,0:T(8,128)}, f32[96,16,128]{2,1,0:T(8,128)}, ...), branch_computations={%region_0.0_spmd, %region_1.5_spmd} | conditional | flops 1243548160 | bytes 294960576 | solution.py:877
  89.6 3.3 %hand_over.1 = (f32[96,16,128]{2,1,0:T(8,128)}, f32[96,32,128]{2,1,0:T(8,128)}) custom-call(f32[96,16,128]{2,1,0:T(8,128)S(1)} %get-tuple-element.18.nest_ref, f32[96,32,128]{2,1,0:T(8,128)S(1)} %get-tuple-element.36.parent_ref), custom_call_target="tpu_custom_call" | custom-call | tf_op jit(solution)/shard_map/cond/branch_0_fun/hand_over/pallas_call | solution.py:856
Async XLA Ops:
  0.6 88.8 %copy-start.6 = (f32[96,32,128]{2,1,0:T(8,128)S(1)}, f32[96,32,128]{2,1,0:T(8,128)}, u32[]{:S(2)}) copy-start(f32[96,32,128]{2,1,0:T(8,128)} %parent_ref.1) | copy-start | bytes 4718596
  0.6 88.8 %copy-start.10 = (f32[96,16,128]{2,1,0:T(8,128)S(1)}, f32[96,16,128]{2,1,0:T(8,128)}, u32[]{:S(2)}) copy-start(f32[96,16,128]{2,1,0:T(8,128)} %nest_ref.1) | copy-start | bytes 2359300
  0.7 88.8 %copy-start.14 = (s32[1,256,81]{1,0,2:T(1,128)S(1)}, s32[1,256,81]{1,0,2:T(1,128)}, u32[]{:S(2)}) copy-start(s32[1,256,81]{1,0,2:T(1,128)} %param.31) | copy-start | bytes 248836
  0.7 88.8 %copy-start.15 = (s32[4,16,128]{2,1,0:T(8,128)S(1)}, s32[4,16,128]{2,1,0:T(8,128)}, u32[]{:S(2)}) copy-start(s32[4,16,128]{2,1,0:T(8,128)} %index_ref.1) | copy-start | bytes 98308
  0.7 88.8 %copy-start.16 = (s32[16,128]{1,0:T(8,128)S(1)}, s32[16,128]{1,0:T(8,128)}, u32[]{:S(2)}) copy-start(s32[16,128]{1,0:T(8,128)} %terrain_ref.1) | copy-start | bytes 24580
  0.7 88.8 %copy-start.17 = (f32[4,16,128]{2,1,0:T(8,128)S(1)}, f32[4,16,128]{2,1,0:T(8,128)}, u32[]{:S(2)}) copy-start(f32[4,16,128]{2,1,0:T(8,128)} %weight_ref.1) | copy-start | bytes 98308
  0.7 88.8 %copy-start.18 = (f32[16,128]{1,0:T(8,128)S(1)}, f32[16,128]{1,0:T(8,128)}, u32[]{:S(2)}) copy-start(f32[16,128]{1,0:T(8,128)} %relax_ref.1) | copy-start | bytes 24580
  0.7 88.8 %copy-start.23 = (s32[1,512]{1,0:T(1,128)S(1)}, s32[1,512]{1,0:T(1,128)}, u32[]{:S(2)}) copy-start(s32[1,512]{1,0:T(1,128)} %fbs_ref.1) | copy-start | bytes 6148
  0.7 88.8 %copy-start.24 = (s32[1,512]{1,0:T(1,128)S(1)}, s32[1,512]{1,0:T(1,128)}, u32[]{:S(2)}) copy-start(s32[1,512]{1,0:T(1,128)} %fbt_ref.1) | copy-start | bytes 6148
  0.7 88.8 %copy-start.26 = (s32[1,256]{1,0:T(1,128)S(1)}, s32[1,256]{1,0:T(1,128)}, u32[]{:S(2)}) copy-start(s32[1,256]{1,0:T(1,128)} %param.27) | copy-start | bytes 3076

commit v3 on v2

--- a/solution.py
+++ b/solution.py
@@ -218,13 +218,20 @@
 
     barrier = pltpu.get_barrier_semaphore()
 
-    def greet(n, carry):
-        tx, ty = chip(n, 1)
+    zs = [lax.rem(mz + k, 4) * 4 for k in range(4)]
+    ys = [lax.rem(my + k, 4) for k in range(4)]
+    xs = [lax.rem(mx + k, 4) * 2 for k in range(4)]
+
+    def ahead(n):
+        dx = n % 4
+        dy = (n // 4 + dx) % 4
+        dz = (n // 16 + dy) % 4
+        return zs[dz] + ys[dy], xs[dx]
+
+    for n in range(1, 64):
+        tx, ty = ahead(n)
         for core in range(2):
             pl.semaphore_signal(barrier, inc=1, device_id=(tx, ty + core), device_id_type=MESH)
-        return carry
-
-    lax.fori_loop(1, 64, greet, 0)
     pl.semaphore_signal(barrier, inc=1, device_id=(gx, mx * 2 + 1 - mc), device_id_type=MESH)
 
     def load(source, count, target, first, k):
@@ -282,20 +289,17 @@
     load(nest_ref, NX, nraw, 0, 1)
     pl.semaphore_wait(barrier, 127)
 
-    def ask(n, carry):
-        tx, ty = chip(n, 1)
+    for n in range(1, 64):
+        tx, ty = ahead(n)
         for core in range(2):
             pltpu.make_async_remote_copy(
                 src_ref=req.at[2 * n + core],
                 dst_ref=reqin.at[2 * n + mc],
                 send_sem=sem_req_s,
-                recv_sem=sem_req_r.at[lax.div(n, 64 // GROUPS)],
+                recv_sem=sem_req_r.at[n // (64 // GROUPS)],
                 device_id=(tx, ty + core),
                 device_id_type=MESH,
             ).start()
-        return carry
-
-    lax.fori_loop(1, 64, ask, 0)
     pltpu.make_async_remote_copy(
         src_ref=req.at[1 - mc],
         dst_ref=reqin.at[mc],
@@ -306,6 +310,11 @@
     ).start()
     pltpu.make_async_copy(req.at[mc], reqin.at[mc], sem_req_r.at[0]).start()
 
+    load(cx_ref, NX, cxs, 0, 2)
+    load(cy_ref, NX, cys, 0, 3)
+    load(cz_ref, NX, czs, 0, 4)
+    load(pcx_ref, PXN, pcxs, 0, 5)
+    load(pcy_ref, PXN, pcys, 0, 6)
 
     lev = lax.broadcasted_iota(jnp.int32, (LEV, 128), 0)
     lane = lax.broadcasted_iota(jnp.int32, (LEV, 128), 1)
@@ -513,11 +522,6 @@
     reply(jnp.int32(1), 3)
     reply(jnp.int32(4), 4)
     lax.fori_loop(1, GROUPS, replies, 0)
-    load(cx_ref, NX, cxs, 0, 2)
-    load(cy_ref, NX, cys, 0, 3)
-    load(cz_ref, NX, czs, 0, 4)
-    load(pcx_ref, PXN, pcxs, 0, 5)
-    load(pcy_ref, PXN, pcys, 0, 6)
 
     for k, (target, count) in enumerate(
         ((cxs, NX), (cys, NX), (czs, NX), (pcxs, PXN), (pcys, PXN))
@@ -674,8 +678,8 @@
     rows = jnp.where(lane512 == LEV, flag, rows)
     fbsend[...] = rows.reshape(128, 4, 128)
 
-    def feed(n, carry):
-        tx, ty = chip(n, 1)
+    for n in range(1, 64):
+        tx, ty = ahead(n)
         for core in range(2):
             pltpu.make_async_remote_copy(
                 src_ref=fbsend.at[tx * 8 + ty + core],
@@ -685,9 +689,6 @@
                 device_id=(tx, ty + core),
                 device_id_type=MESH,
             ).start()
-        return carry
-
-    lax.fori_loop(1, 64, feed, 0)
     other = mx * 2 + 1 - mc
     pltpu.make_async_remote_copy(
         src_ref=fbsend.at[gx * 8 + other],

time: 93.5 us -> 92.8 us (level)
  no operation moved by 1% of the time
where the time goes in v3:
time: 92.8 us; the launch traced here: 92.6 us
  Pallas kernels  90.6 us (98%)
  between operations  1.69 us (2%)
    pallas_call x1, Pallas kernels, fused_step(): pl.pallas_call(step_kernel, out_shape=(jax.ShapeDtypeStruct(nest_field.sh...  87.3 us
    pallas_call x1, Pallas kernels, handed(): pl.pallas_call(hand_over, out_shape=(jax.ShapeDtypeStruct(nest_out.shape,...  3.29 us

profile of v3, /device:TPU:1, one launch (start us, length us, event | category | flops | bytes accessed | tf_op | source)
XLA Modules:
  0.0 92.6 jit_solution(6913250317863509505)
XLA Ops:
  0.6 0.0 copy-start.6
  0.6 0.0 copy-start.10
  0.7 0.0 copy-start.14
  0.7 0.0 copy-start.15
  0.7 0.0 copy-start.16
  0.7 0.0 copy-start.17
  0.7 0.0 copy-start.18
  0.7 0.0 copy-start.23
  0.7 0.0 copy-start.24
  0.7 0.0 copy-start.26
  0.7 87.3 %step.1 = (f32[96,16,128]{2,1,0:T(8,128)S(1)}, f32[96,32,128]{2,1,0:T(8,128)S(1)}, s32[1]{0:T(128)}) custom-call(s32[256]{0:T(256)} %bitcast.82, f32[96,16,128]{2,1,0:T(8,128)} %nest_ref.1, f32[96,16,128]{2,1,0:T(8,128)} %cx_ref.1, f32[96,16,128]{2,1,0:T(8,128)} %cy_ref.1, f32[96,16,128]{2,1,0:T(8,128)} %cz_ref.1, s32[16,128]{1,0:T(8,128)} %terrain_ref.1, ...), custom_call_target="tpu_custom_call" | custom-call | tf_op jit(solution)/shard_map/step/pallas_call | solution.py:802
  88.7 0.0 copy-done.6
  88.7 0.0 copy-done.10
  88.7 0.0 copy-done.14
  88.7 0.0 copy-done.15
  88.7 0.0 copy-done.16
  88.7 0.0 copy-done.17
  88.8 0.0 copy-done.18
  88.8 0.0 copy-done.23
  88.8 0.0 copy-done.24
  88.8 0.0 copy-done.26
  88.8 3.6 %conditional.1 = ((f32[96,16,128]{2,1,0:T(8,128)}, f32[96,32,128]{2,1,0:T(8,128)})) conditional(s32[]{:T(128)} %bitcast.31, (f32[96,16,128]{2,1,0:T(8,128)S(1)}, f32[96,32,128]{2,1,0:T(8,128)S(1)}) %tuple.15, (s32[16,128]{1,0:T(8,128)S(1)}, f32[96,16,128]{2,1,0:T(8,128)S(1)}, f32[96,16,128]{2,1,0:T(8,128)}, f32[96,16,128]{2,1,0:T(8,128)}, ...), branch_computations={%region_0.0_spmd, %region_1.5_spmd} | conditional | flops 1243548160 | bytes 294960576 | solution.py:878
  88.8 3.3 %hand_over.1 = (f32[96,16,128]{2,1,0:T(8,128)}, f32[96,32,128]{2,1,0:T(8,128)}) custom-call(f32[96,16,128]{2,1,0:T(8,128)S(1)} %get-tuple-element.18.nest_ref, f32[96,32,128]{2,1,0:T(8,128)S(1)} %get-tuple-element.36.parent_ref), custom_call_target="tpu_custom_call" | custom-call | tf_op jit(solution)/shard_map/cond/branch_0_fun/hand_over/pallas_call | solution.py:857
Async XLA Ops:
  0.6 88.1 %copy-start.6 = (f32[96,32,128]{2,1,0:T(8,128)S(1)}, f32[96,32,128]{2,1,0:T(8,128)}, u32[]{:S(2)}) copy-start(f32[96,32,128]{2,1,0:T(8,128)} %parent_ref.1) | copy-start | bytes 4718596
  0.6 88.1 %copy-start.10 = (f32[96,16,128]{2,1,0:T(8,128)S(1)}, f32[96,16,128]{2,1,0:T(8,128)}, u32[]{:S(2)}) copy-start(f32[96,16,128]{2,1,0:T(8,128)} %nest_ref.1) | copy-start | bytes 2359300
  0.7 88.1 %copy-start.14 = (s32[1,256,81]{1,0,2:T(1,128)S(1)}, s32[1,256,81]{1,0,2:T(1,128)}, u32[]{:S(2)}) copy-start(s32[1,256,81]{1,0,2:T(1,128)} %param.31) | copy-start | bytes 248836
  0.7 88.1 %copy-start.15 = (s32[4,16,128]{2,1,0:T(8,128)S(1)}, s32[4,16,128]{2,1,0:T(8,128)}, u32[]{:S(2)}) copy-start(s32[4,16,128]{2,1,0:T(8,128)} %index_ref.1) | copy-start | bytes 98308
  0.7 88.1 %copy-start.16 = (s32[16,128]{1,0:T(8,128)S(1)}, s32[16,128]{1,0:T(8,128)}, u32[]{:S(2)}) copy-start(s32[16,128]{1,0:T(8,128)} %terrain_ref.1) | copy-start | bytes 24580
  0.7 88.1 %copy-start.17 = (f32[4,16,128]{2,1,0:T(8,128)S(1)}, f32[4,16,128]{2,1,0:T(8,128)}, u32[]{:S(2)}) copy-start(f32[4,16,128]{2,1,0:T(8,128)} %weight_ref.1) | copy-start | bytes 98308
  0.7 88.1 %copy-start.18 = (f32[16,128]{1,0:T(8,128)S(1)}, f32[16,128]{1,0:T(8,128)}, u32[]{:S(2)}) copy-start(f32[16,128]{1,0:T(8,128)} %relax_ref.1) | copy-start | bytes 24580
  0.7 88.1 %copy-start.23 = (s32[1,512]{1,0:T(1,128)S(1)}, s32[1,512]{1,0:T(1,128)}, u32[]{:S(2)}) copy-start(s32[1,512]{1,0:T(1,128)} %fbs_ref.1) | copy-start | bytes 6148
  0.7 88.1 %copy-start.24 = (s32[1,512]{1,0:T(1,128)S(1)}, s32[1,512]{1,0:T(1,128)}, u32[]{:S(2)}) copy-start(s32[1,512]{1,0:T(1,128)} %fbt_ref.1) | copy-start | bytes 6148
  0.7 88.1 %copy-start.26 = (s32[1,256]{1,0:T(1,128)S(1)}, s32[1,256]{1,0:T(1,128)}, u32[]{:S(2)}) copy-start(s32[1,256]{1,0:T(1,128)} %param.27) | copy-start | bytes 3076
